TPU v7x, 512 devices: a whole 4x4x16 slice. The times are simulated.
512 devices in a mesh: row: 16 (over y, x), col: 32 (over z, core).
Axes of the slice: x: 4, y: 4, z: 16, core: 2. Of those that a mesh axis runs over, the one named last changes fastest.
Arguments:
- points: bfloat16 [262144, 256], P(('col', 'row')), may hold values from -6 to 6
- weights: bfloat16 [262144, 128], P(('col', 'row')), may hold values from -6 to 6
- near_blocks: int32 [2048, 16], P(('col', 'row')), may hold values from 0 to 2047, as said below
- proxies: bfloat16 [64, 256], replicated, may hold values from -6 to 6
Outputs:
- near_product: bfloat16 [262144, 128], P(('col', 'row'))
- factors: float32 [32768, 192], P(('col', 'row'))
Inputs may be any that keep to these rules, and one draw needn't show every extreme that they name: near_blocks[j, 0] = j; every entry of row j lies in the column group of j, that is in the same run of 64 blocks; entries may repeat.
All inputs are finite; a program needn't handle non-finite values.
Results may differ from a plain program's by a relative error of at most 0.01.
Values may be sent and summed in bfloat16 or wider, within the bound.
No kernel may reach another device: no remote copies, remote signals or barrier semaphores. Data moves between devices by JAX's collectives and lax.ppermute only.
A program may use at most 64 MiB of HBM per device.

v0:
```python
import jax
import jax.numpy as jnp
from jax import lax
from jax.sharding import PartitionSpec as P

DIM = 256
BLK = 128
NV = 128


def partner(value, axis, stride):
    mask = 2**stride
    pairs = [(source, source ^ mask) for source in range(lax.axis_size(axis))]
    return lax.ppermute(value, axis, pairs)


def kern_tile(left, right):
    cross = jnp.dot(left, right.T, preferred_element_type=jnp.float32)
    lnorm = jnp.sum(left.astype(jnp.float32) ** 2, axis=-1)
    rnorm = jnp.sum(right.astype(jnp.float32) ** 2, axis=-1)
    return jnp.exp(-(lnorm[:, None] + rnorm[None, :] - 2.0 * cross) * (2.0 / DIM))


def level_merge(lower_own, lower_other):
    high = lax.Precision.HIGHEST
    gram = jnp.dot(lower_own, lower_own.T, precision=high) + jnp.dot(
        lower_other, lower_other.T, precision=high
    )
    merged = jnp.linalg.cholesky(gram)
    transfer = lax.linalg.triangular_solve(merged, lower_own, left_side=True, lower=True).T
    return (merged, transfer)


def on_device(points, weights, near_blocks, proxies):
    n_local = near_blocks.shape[0]
    group_count = n_local * lax.axis_size("row")
    base = lax.axis_index("col") * group_count
    gathered = lax.all_gather(points, "row", axis=0, tiled=True)
    tblocks = gathered.reshape(group_count, BLK, DIM)
    local_ids = near_blocks - base
    sources = points.reshape(n_local, BLK, DIM)
    wblocks = weights.reshape(n_local, BLK, NV)
    targets = tblocks[local_ids]
    cross = jnp.einsum("jtad,jbd->jtab", targets, sources, preferred_element_type=jnp.float32)
    tnorm = jnp.sum(targets.astype(jnp.float32) ** 2, axis=-1)
    snorm = jnp.sum(sources.astype(jnp.float32) ** 2, axis=-1)
    dist = tnorm[:, :, :, None] + snorm[:, None, None, :] - 2.0 * cross
    tile = jnp.exp(-dist * (2.0 / DIM)).astype(jnp.bfloat16)
    contrib = jnp.einsum("jtab,jbv->jtav", tile, wblocks, preferred_element_type=jnp.float32)
    partial_value = jnp.zeros((group_count, BLK, NV), jnp.float32)
    partial_value = partial_value.at[local_ids.reshape(-1)].add(contrib.reshape(-1, BLK, NV))
    near_sum = lax.psum_scatter(
        partial_value.reshape(group_count * BLK, NV), "row", scatter_dimension=0, tiled=True
    )
    near_product = near_sum.astype(jnp.bfloat16)
    far = kern_tile(points, proxies)
    lower0 = jnp.linalg.cholesky(jnp.dot(far.T, far, precision=lax.Precision.HIGHEST))
    current = lower0
    transfers = []
    for level in range(2):
        sibling = partner(current, "col", level)
        current, transfer = level_merge(current, sibling)
        transfers.append(transfer)
    factors = jnp.concatenate([transfers[0], transfers[1], current.T], axis=1)
    return (near_product, factors)


def solution(mesh):
    placed = (P(("col", "row"), None), P(("col", "row"), None), P(("col", "row"), None), P())
    return jax.shard_map(
        on_device,
        mesh=mesh,
        in_specs=placed,
        out_specs=(P(("col", "row"), None), P(("col", "row"), None)),
        check_vma=False,
    )
```

profile of v0, /device:TPU:2, one launch (start us, length us, event | category | flops | bytes accessed | tf_op | source)
XLA Modules:
  0.0 213.1 jit_solution(5560618731934013219)
XLA Ops:
  7.2 0.7 all-gather.2.cloned.1.call-update
  8.0 0.7 compare_select_fusion
  8.8 1.1 multiply_reduce_fusion.1
  9.9 72.4 %all-gather.2.cloned.1.call-done = bf16[8192,256]{1,0:T(8,128)(2,1)} async-done(((bf16[512,256]{1,0:T(8,128)(2,1)}), bf16[8192,256]{1,0:T(8,128)(2,1)}) %all-gather.2.cloned.1.call-update) | async-done | bytes 4194320 | tf_op jit(solution)/shard_map/all_gather | solution.py:38
  82.4 5.0 %gather_fusion = bf16[64,128,256]{2,1,0:T(8,128)(2,1)} fusion(bf16[64,128,256]{2,1,0:T(8,128)(2,1)} %bitcast.66, s32[1024]{0:T(1024)S(1)} %pad_clamp_fusion), kind=kCustom, calls=%fused_computation | custom fusion | bytes 8388864 | tf_op jit(solution)/shard_map/gather | solution.py:43
  87.3 3.4 %multiply_reduce_fusion = f32[4,16,128]{2,1,0:T(8,128)S(1)} fusion(bf16[4,16,128,256]{3,2,1,0:T(8,128)(2,1)} %bitcast.64), kind=kLoop, calls=%fused_computation.2 | loop fusion | flops 6283264 | bytes 4227072 | tf_op jit(solution)/shard_map/reduce_sum | solution.py:45
  90.7 4.9 %fusion = f32[4,16,128,128]{3,2,1,0:T(8,128)} fusion(bf16[4,128,128,1]{2,1,3,0:T(8,128)(2,1)S(1)} %bitcast.62, bf16[4,16,128,256]{3,2,1,0:T(8,128)(2,1)} %bitcast.65, bf16[4,128,256,1]{2,1,3,0:T(8,128)(2,1)S(1)} %bitcast.68, f32[4,128]{1,0:T(4,128)S(1)} %bitcast.69, f32[4,16,128]{2,1,0:T(8,128)S(1)} %multiply_reduce_fusion), kind=kOutput, calls=%fused_computation.4 | convolution fusion | flops 811597824 | bytes 8816640 | tf_op jit(solution)/shard_map/jtab,jbv->jtav/dot_general | solution.py:49
  95.6 2.5 %broadcast_in_dim.4 = f32[64,128,128]{2,1,0:T(8,128)} broadcast(f32[]{:T(128)} %constant.43.clone.1), dimensions={} | broadcast | bytes 4194308 | tf_op jit(solution)/shard_map/broadcast_in_dim | solution.py:50
  98.1 13.6 %scatter_fusion = f32[64,128,128]{2,1,0:T(8,128)} fusion(f32[64,128,128]{2,1,0:T(8,128)} %broadcast_in_dim.4, s32[64]{0:T(128)S(1)} %fusion.15, f32[64,128,128]{2,1,0:T(8,128)} %bitcast.67), kind=kCustom, calls=%fused_computation.1 | custom fusion | flops 1048576 | bytes 12583168 | tf_op jit(solution)/shard_map/scatter-add | solution.py:51
  111.8 0.7 copy-done.2
  113.6 5.8 %cholesky.59 = f32[64,64]{1,0:T(8,128)S(1)} custom-call(f32[64,64]{1,0:T(8,128)S(1)} %fusion.9), custom_call_target="Cholesky" | custom-call | tf_op jit(solution)/shard_map/jit(cholesky)/cholesky | solution.py:57
  120.1 0.7 fusion.10
  120.8 1.9 collective-permute-start
  122.9 1.0 collective-permute-done
  124.2 5.8 %cholesky.70 = f32[64,64]{1,0:T(8,128)S(1)} custom-call(f32[64,64]{1,0:T(8,128)S(1)} %fusion.8), custom_call_target="Cholesky" | custom-call | tf_op jit(solution)/shard_map/jit(cholesky)/cholesky | solution.py:29
  130.7 0.7 select_bitcast_fusion.1
  131.3 3.3 %collective-permute-start.1 = (f32[64,64]{1,0:T(8,128)S(1)}, f32[64,64]{1,0:T(8,128)S(1)}, u32[]{:S(2)}, u32[]{:S(2)}) collective-permute-start(f32[64,64]{1,0:T(8,128)S(1)} %get-tuple-element.7), channel_id=1, source_target_pairs={{0,2},{1,3},{2,0},{3,1},{4,6},{5,7},{6,4},{7,5},{8,10},{9,11},{10,... | collective-permute-start | bytes 49160 | tf_op jit(solution)/shard_map/ppermute | solution.py:14
  134.7 4.9 %custom-call.6 = f32[1,64,64]{1,2,0:T(8,128)S(1)} custom-call(f32[1,64,64]{2,1,0:T(8,128)S(1)} %get-tuple-element.6), custom_call_target="InvertDiagBlocksLowerTriangular" | custom-call | tf_op jit(solution)/shard_map/triangular_solve/custom-call.0 | solution.py:30
  140.3 5.8 %cholesky.81 = f32[64,64]{1,0:T(8,128)S(1)} custom-call(f32[64,64]{1,0:T(8,128)S(1)} %fusion.6), custom_call_target="Cholesky" | custom-call | tf_op jit(solution)/shard_map/jit(cholesky)/cholesky | solution.py:29
  146.8 0.7 select_bitcast_fusion
  147.5 4.9 %custom-call.7 = f32[1,64,64]{1,2,0:T(8,128)S(1)} custom-call(f32[1,64,64]{2,1,0:T(8,128)S(1)} %get-tuple-element.10), custom_call_target="InvertDiagBlocksLowerTriangular" | custom-call | tf_op jit(solution)/shard_map/triangular_solve/custom-call.0 | solution.py:30
  152.7 0.7 copy.15
  153.4 51.3 %reduce-scatter.2.cloned.1.call-done = f32[512,128]{1,0:T(8,128)} async-done(((f32[8192,128]{1,0:T(8,128)}), f32[512,128]{1,0:T(8,128)}) %reduce-scatter.2.cloned.1.call-update) | async-done | bytes 262160 | tf_op jit(solution)/shard_map/reduce_scatter | solution.py:52
  204.7 1.6 convert_element_type.20
  (35 shorter events, 4.7 us)
Async XLA Ops:
  7.2 83.6 %copy-start = (bf16[512,128]{1,0:T(8,128)(2,1)S(1)}, bf16[512,128]{1,0:T(8,128)(2,1)}, u32[]{:S(2)}) copy-start(bf16[512,128]{1,0:T(8,128)(2,1)} %param.8) | copy-start | bytes 393220
  7.2 75.2 %all-gather.2.cloned.1.call-start = ((), (), s32[]{:S(2)}) async-start(), calls=%async_computation.1 | async-start | bytes 4456448 | tf_op jit(solution)/shard_map/all_gather | solution.py:38
  7.9 196.8 %reduce-scatter.2.cloned.1.call-start = ((), (), s32[]{:S(2)}) async-start(), calls=%async_computation.2 | async-start | bytes 4456448 | tf_op jit(solution)/shard_map/reduce_scatter | solution.py:52
  87.3 3.4 %copy-start.1 = (bf16[512,256]{1,0:T(8,128)(2,1)S(1)}, bf16[512,256]{1,0:T(8,128)(2,1)}, u32[]{:S(2)}) copy-start(bf16[512,256]{1,0:T(8,128)(2,1)} %param.7) | copy-start | bytes 786436
  111.8 0.8 copy-start.2
  120.8 3.1 %collective-permute-start = (f32[64,64]{1,0:T(8,128)S(1)}, f32[64,64]{1,0:T(8,128)S(1)}, u32[]{:S(2)}, u32[]{:S(2)}) collective-permute-start(f32[64,64]{1,0:T(8,128)S(1)} %fusion.10), channel_id=1, source_target_pairs={{0,1},{1,0},{2,3},{3,2},{4,5},{5,4},{6,7},{7,6},{8,9},{9,8},{10,11... | collective-permute-start | bytes 49160 | tf_op jit(solution)/shard_map/ppermute | solution.py:14
  131.3 8.7 %collective-permute-start.1 = (f32[64,64]{1,0:T(8,128)S(1)}, f32[64,64]{1,0:T(8,128)S(1)}, u32[]{:S(2)}, u32[]{:S(2)}) collective-permute-start(f32[64,64]{1,0:T(8,128)S(1)} %get-tuple-element.7), channel_id=1, source_target_pairs={{0,2},{1,3},{2,0},{3,1},{4,6},{5,7},{6,4},{7,5},{8,10},{9,11},{10,... | collective-permute-start | bytes 49160 | tf_op jit(solution)/shard_map/ppermute | solution.py:14
Sparse Core Ops, SparseCore 0:
  11.0 71.2 all-gather.1
  111.9 92.7 reduce-scatter.1
where the time goes:
time: 214 us; the launch traced here: 213 us
  waiting for transfers between devices  125 us (58%)
  other arithmetic  51.9 us (24%)
  between operations  14.3 us (7%)
  local copies, waits for them, and re-layouts  9.3 us (4%)
  matrix products  6.97 us (3%)
  starting transfers between devices  5.31 us (2%)
    all_gather x1, waiting for transfers between devices, on_device(): gathered = lax.all_gather(points, 'row', axis=0, tiled=True)  72.4 us
    reduce_scatter x1, waiting for transfers between devices, on_device(): lax.psum_scatter(partial_value.reshape(group_count * BLK, NV), 'row', sca...  51.3 us
    scatter-add x1, other arithmetic, on_device(): partial_value.at[local_ids.reshape(-1)].add(contrib.reshape(-1, BLK, NV))  13.6 us
    another operation x6, other arithmetic, level_merge(): merged = jnp.linalg.cholesky(gram)  13 us
    another operation x4, other arithmetic, level_merge(): lax.linalg.triangular_solve(merged, lower_own, left_side=True, lower=True)  11.1 us
    another operation x3, other arithmetic, on_device(): jnp.linalg.cholesky(jnp.dot(far.T, far, precision=lax.Precision.HIGHEST))  6.52 us
    ppermute x2, starting transfers between devices, partner(): return lax.ppermute(value, axis, pairs)  5.24 us
    gather x1, local copies, waits for them, and re-layouts, on_device(): targets = tblocks[local_ids]  4.97 us
  transfers between devices with their start and end apart: 4, of which 3 were waited for; matrix products, arithmetic and copies ran while one was open for 17% of the time, Pallas kernels for 0%

commit v1 on v0

--- a/solution.py
+++ b/solution.py
@@ -1,11 +1,37 @@
+import functools
 import jax
 import jax.numpy as jnp
 from jax import lax
 from jax.sharding import PartitionSpec as P
+from jax.lax import axis_index, axis_size, ppermute
 
 DIM = 256
 BLK = 128
 NV = 128
+
+
+def replace_results(a0, d_out):
+    passed, work_now, n_now = (axis_size("row"), axis_index("row"), a0.shape[d_out])
+    pieces_in = [(u, (u + 1) % passed) for u in range(passed)]
+    top = jnp.zeros((*a0.shape[:d_out], passed * n_now, *a0.shape[d_out + 1 :]), a0.dtype)
+    by_place = [(u, (u - 1) % passed) for u in range(passed)]
+    v_now = block_last = a0
+    top = lax.dynamic_update_slice_in_dim(top, a0, work_now * n_now, axis=d_out)
+    plain = passed // 2
+    for kk in range(1, plain + 1):
+        v_now = ppermute(v_now, "row", perm=pieces_in)
+        top = lax.dynamic_update_slice_in_dim(
+            top, v_now, (work_now - kk) % passed * n_now, axis=d_out
+        )
+        if kk < passed - plain:
+            block_last = ppermute(block_last, "row", by_place)
+            top = lax.dynamic_update_slice_in_dim(
+                top, block_last, (work_now + kk) % passed * n_now, axis=d_out
+            )
+    return top
+
+
+work_series_all = functools.partial(replace_results, d_out=0)
 
 
 def partner(value, axis, stride):
@@ -35,7 +61,7 @@
     n_local = near_blocks.shape[0]
     group_count = n_local * lax.axis_size("row")
     base = lax.axis_index("col") * group_count
-    gathered = lax.all_gather(points, "row", axis=0, tiled=True)
+    gathered = work_series_all(points)
     tblocks = gathered.reshape(group_count, BLK, DIM)
     local_ids = near_blocks - base
     sources = points.reshape(n_local, BLK, DIM)

time: 214 us -> 237 us (1.11)
  starting transfers between devices: 5.31 us -> 70.9 us
  waiting for transfers between devices: 125 us -> 68.3 us
  local copies, waits for them, and re-layouts: 9.3 us -> 23.2 us
    all_gather x1 -> x0, waiting for transfers between devices: 72.4 us -> none  [on_device(): gathered = lax.all_gather(points, 'row', axis=0, tiled=True)]
    ppermute x0 -> x15, starting transfers between devices: none -> 66.9 us  [the longest x7 50 us: replace_results(): block_last = ppermute(block_last, 'row', by_place)]
    ppermute x0 -> x15, waiting for transfers between devices: none -> 20.2 us  [the longest x8 20.2 us: replace_results(): v_now = ppermute(v_now, 'row', perm=pieces_in)]
    dynamic_update_slice x0 -> x16, local copies, waits for them, and re-layouts: none -> 11.7 us  [the longest x8 5.81 us: replace_results(): lax.dynamic_update_slice_in_dim(top, v_now, (work_now - kk) % passed * n_...]
    reduce_scatter x1, waiting for transfers between devices: 51.3 us -> 47.1 us  [on_device(): lax.psum_scatter(partial_value.reshape(group_count * BLK, NV), 'row', sca...]
  transfers between devices with their start and end apart: 4 -> 18, of which waited for: 3 -> 9; matrix products, arithmetic and copies ran while one was open for 17% -> 21% of each run, Pallas kernels for 0% -> 0%
where the time goes in v1:
time: 237 us; the launch traced here: 236 us
  starting transfers between devices  70.9 us (30%)
  waiting for transfers between devices  68.3 us (29%)
  other arithmetic  51.9 us (22%)
  local copies, waits for them, and re-layouts  23.2 us (10%)
  between operations  14.7 us (6%)
  matrix products  6.96 us (3%)
    ppermute x7, starting transfers between devices, replace_results(): block_last = ppermute(block_last, 'row', by_place)  50 us
    reduce_scatter x1, waiting for transfers between devices, on_device(): lax.psum_scatter(partial_value.reshape(group_count * BLK, NV), 'row', sca...  47.1 us
    ppermute x8, waiting for transfers between devices, replace_results(): v_now = ppermute(v_now, 'row', perm=pieces_in)  20.2 us
    ppermute x8, starting transfers between devices, replace_results(): v_now = ppermute(v_now, 'row', perm=pieces_in)  16.9 us
    scatter-add x1, other arithmetic, on_device(): partial_value.at[local_ids.reshape(-1)].add(contrib.reshape(-1, BLK, NV))  13.6 us
    another operation x6, other arithmetic, level_merge(): merged = jnp.linalg.cholesky(gram)  13 us
    another operation x4, other arithmetic, level_merge(): lax.linalg.triangular_solve(merged, lower_own, left_side=True, lower=True)  11.1 us
    another operation x3, other arithmetic, on_device(): jnp.linalg.cholesky(jnp.dot(far.T, far, precision=lax.Precision.HIGHEST))  6.52 us
  transfers between devices with their start and end apart: 18, of which 9 were waited for; matrix products, arithmetic and copies ran while one was open for 21% of the time, Pallas kernels for 0%

profile of v1, /device:TPU:2, one launch (start us, length us, event | category | flops | bytes accessed | tf_op | source)
XLA Modules:
  0.0 235.8 jit_solution(11581368593372789796)
XLA Ops:
  7.2 3.5 %collective-permute-start = (bf16[512,256]{1,0:T(8,128)(2,1)}, bf16[512,256]{1,0:T(8,128)(2,1)S(1)}, u32[]{:S(2)}, u32[]{:S(2)}) collective-permute-start(bf16[512,256]{1,0:T(8,128)(2,1)} %param.7), channel_id=1, source_target_pairs={{0,32},{32,64},{64,96},{96,128},{128,160},{160,192},{192,224},{224... | collective-permute-start | bytes 786440 | tf_op jit(solution)/shard_map/ppermute | solution.py:22
  10.8 6.3 %collective-permute-start.1 = (bf16[512,256]{1,0:T(8,128)(2,1)}, bf16[512,256]{1,0:T(8,128)(2,1)S(1)}, u32[]{:S(2)}, u32[]{:S(2)}) collective-permute-start(bf16[512,256]{1,0:T(8,128)(2,1)} %param.7), channel_id=1, source_target_pairs={{0,480},{32,0},{64,32},{96,64},{128,96},{160,128},{192,160},{224,1... | collective-permute-start | bytes 786440 | tf_op jit(solution)/shard_map/ppermute | solution.py:27
  17.1 2.6 %collective-permute-done = bf16[512,256]{1,0:T(8,128)(2,1)S(1)} collective-permute-done((bf16[512,256]{1,0:T(8,128)(2,1)}, bf16[512,256]{1,0:T(8,128)(2,1)S(1)}, u32[]{:S(2)}, u32[]{:S(2)}) %collective-permute-start) | collective-permute-done | bytes 262176 | tf_op jit(solution)/shard_map/ppermute | solution.py:22
  22.4 7.2 %collective-permute-start.3 = (bf16[512,256]{1,0:T(8,128)(2,1)S(1)}, bf16[512,256]{1,0:T(8,128)(2,1)S(1)}, u32[]{:S(2)}, u32[]{:S(2)}) collective-permute-start(bf16[512,256]{1,0:T(8,128)(2,1)S(1)} %collective-permute-done.1), channel_id=1, source_target_pairs={{0,480},{32,0},{64,32},{96,64},{128,96},{160,128},{192,160},{224,1... | collective-permute-start | bytes 786440 | tf_op jit(solution)/shard_map/ppermute | solution.py:27
  34.4 7.2 %collective-permute-start.5 = (bf16[512,256]{1,0:T(8,128)(2,1)S(1)}, bf16[512,256]{1,0:T(8,128)(2,1)S(1)}, u32[]{:S(2)}, u32[]{:S(2)}) collective-permute-start(bf16[512,256]{1,0:T(8,128)(2,1)S(1)} %collective-permute-done.3), channel_id=1, source_target_pairs={{0,480},{32,0},{64,32},{96,64},{128,96},{160,128},{192,160},{224,1... | collective-permute-start | bytes 786440 | tf_op jit(solution)/shard_map/ppermute | solution.py:27
  41.6 2.2 broadcast_in_dim.7
  47.5 7.2 %collective-permute-start.7 = (bf16[512,256]{1,0:T(8,128)(2,1)S(1)}, bf16[512,256]{1,0:T(8,128)(2,1)S(1)}, u32[]{:S(2)}, u32[]{:S(2)}) collective-permute-start(bf16[512,256]{1,0:T(8,128)(2,1)S(1)} %collective-permute-done.5), channel_id=1, source_target_pairs={{0,480},{32,0},{64,32},{96,64},{128,96},{160,128},{192,160},{224,1... | collective-permute-start | bytes 786440 | tf_op jit(solution)/shard_map/ppermute | solution.py:27
  60.8 7.5 %collective-permute-start.9 = (bf16[512,256]{1,0:T(8,128)(2,1)S(1)}, bf16[512,256]{1,0:T(8,128)(2,1)S(1)}, u32[]{:S(2)}, u32[]{:S(2)}) collective-permute-start(bf16[512,256]{1,0:T(8,128)(2,1)S(1)} %collective-permute-done.7), channel_id=1, source_target_pairs={{0,480},{32,0},{64,32},{96,64},{128,96},{160,128},{192,160},{224,1... | collective-permute-start | bytes 786440 | tf_op jit(solution)/shard_map/ppermute | solution.py:27
  69.1 2.8 %collective-permute-done.8 = bf16[512,256]{1,0:T(8,128)(2,1)S(1)} collective-permute-done((bf16[512,256]{1,0:T(8,128)(2,1)S(1)}, bf16[512,256]{1,0:T(8,128)(2,1)S(1)}, u32[]{:S(2)}, u32[]{:S(2)}) %collective-permute-start.8) | collective-permute-done | bytes 262176 | tf_op jit(solution)/shard_map/ppermute | solution.py:22
  75.2 7.4 %collective-permute-start.11 = (bf16[512,256]{1,0:T(8,128)(2,1)S(1)}, bf16[512,256]{1,0:T(8,128)(2,1)S(1)}, u32[]{:S(2)}, u32[]{:S(2)}) collective-permute-start(bf16[512,256]{1,0:T(8,128)(2,1)S(1)} %collective-permute-done.9), channel_id=1, source_target_pairs={{0,480},{32,0},{64,32},{96,64},{128,96},{160,128},{192,160},{224,1... | collective-permute-start | bytes 786440 | tf_op jit(solution)/shard_map/ppermute | solution.py:27
  83.4 2.4 %collective-permute-done.10 = bf16[512,256]{1,0:T(8,128)(2,1)S(1)} collective-permute-done((bf16[512,256]{1,0:T(8,128)(2,1)S(1)}, bf16[512,256]{1,0:T(8,128)(2,1)S(1)}, u32[]{:S(2)}, u32[]{:S(2)}) %collective-permute-start.10) | collective-permute-done | bytes 262176 | tf_op jit(solution)/shard_map/ppermute | solution.py:22
  89.2 7.0 %collective-permute-start.13 = (bf16[512,256]{1,0:T(8,128)(2,1)S(1)}, bf16[512,256]{1,0:T(8,128)(2,1)S(1)}, u32[]{:S(2)}, u32[]{:S(2)}) collective-permute-start(bf16[512,256]{1,0:T(8,128)(2,1)S(1)} %collective-permute-done.11), channel_id=1, source_target_pairs={{0,480},{32,0},{64,32},{96,64},{128,96},{160,128},{192,160},{224,1... | collective-permute-start | bytes 786440 | tf_op jit(solution)/shard_map/ppermute | solution.py:27
  102.7 7.2 %collective-permute-done.14 = bf16[512,256]{1,0:T(8,128)(2,1)S(1)} collective-permute-done((bf16[512,256]{1,0:T(8,128)(2,1)S(1)}, bf16[512,256]{1,0:T(8,128)(2,1)S(1)}, u32[]{:S(2)}, u32[]{:S(2)}) %collective-permute-start.14) | collective-permute-done | bytes 262176 | tf_op jit(solution)/shard_map/ppermute | solution.py:22
  110.6 5.0 %gather_fusion = bf16[64,128,256]{2,1,0:T(8,128)(2,1)} fusion(bf16[64,128,256]{2,1,0:T(8,128)(2,1)} %bitcast.1, s32[1024]{0:T(1024)S(1)} %pad_clamp_fusion), kind=kCustom, calls=%fused_computation | custom fusion | bytes 8388864 | tf_op jit(solution)/shard_map/gather | solution.py:69
  115.5 3.3 %multiply_reduce_fusion = f32[4,16,128]{2,1,0:T(8,128)S(1)} fusion(bf16[4,16,128,256]{3,2,1,0:T(8,128)(2,1)} %bitcast.64), kind=kLoop, calls=%fused_computation.2 | loop fusion | flops 6283264 | bytes 4227072 | tf_op jit(solution)/shard_map/reduce_sum | solution.py:71
  118.9 4.9 %fusion = f32[4,16,128,128]{3,2,1,0:T(8,128)} fusion(bf16[4,128,128,1]{2,1,3,0:T(8,128)(2,1)S(1)} %bitcast.62, bf16[4,16,128,256]{3,2,1,0:T(8,128)(2,1)} %bitcast.65, bf16[4,128,256,1]{2,1,3,0:T(8,128)(2,1)S(1)} %bitcast.67, f32[4,128]{1,0:T(4,128)S(1)} %bitcast.68, f32[4,16,128]{2,1,0:T(8,128)S(1)} %multiply_reduce_fusion), kind=kOutput, calls=%fused_computation.4 | convolution fusion | flops 811597824 | bytes 8816640 | tf_op jit(solution)/shard_map/jtab,jbv->jtav/dot_general | solution.py:75
  123.8 2.5 %broadcast_in_dim.6 = f32[64,128,128]{2,1,0:T(8,128)} broadcast(f32[]{:T(128)} %constant.132.clone.1), dimensions={} | broadcast | bytes 4194308 | tf_op jit(solution)/shard_map/broadcast_in_dim | solution.py:76
  126.3 13.6 %scatter_fusion = f32[64,128,128]{2,1,0:T(8,128)} fusion(f32[64,128,128]{2,1,0:T(8,128)} %broadcast_in_dim.6, s32[64]{0:T(128)S(1)} %fusion.15, f32[64,128,128]{2,1,0:T(8,128)} %bitcast.66), kind=kCustom, calls=%fused_computation.1 | custom fusion | flops 1048576 | bytes 12583168 | tf_op jit(solution)/shard_map/scatter-add | solution.py:77
  141.7 5.8 %cholesky.59 = f32[64,64]{1,0:T(8,128)S(1)} custom-call(f32[64,64]{1,0:T(8,128)S(1)} %fusion.9), custom_call_target="Cholesky" | custom-call | tf_op jit(solution)/shard_map/jit(cholesky)/cholesky | solution.py:83
  152.3 5.8 %cholesky.70 = f32[64,64]{1,0:T(8,128)S(1)} custom-call(f32[64,64]{1,0:T(8,128)S(1)} %fusion.8), custom_call_target="Cholesky" | custom-call | tf_op jit(solution)/shard_map/jit(cholesky)/cholesky | solution.py:55
  161.6 4.9 %custom-call.6 = f32[1,64,64]{1,2,0:T(8,128)S(1)} custom-call(f32[1,64,64]{2,1,0:T(8,128)S(1)} %get-tuple-element.6), custom_call_target="InvertDiagBlocksLowerTriangular" | custom-call | tf_op jit(solution)/shard_map/triangular_solve/custom-call.0 | solution.py:56
  167.2 5.8 %cholesky.81 = f32[64,64]{1,0:T(8,128)S(1)} custom-call(f32[64,64]{1,0:T(8,128)S(1)} %fusion.6), custom_call_target="Cholesky" | custom-call | tf_op jit(solution)/shard_map/jit(cholesky)/cholesky | solution.py:55
  174.4 4.9 %custom-call.7 = f32[1,64,64]{1,2,0:T(8,128)S(1)} custom-call(f32[1,64,64]{2,1,0:T(8,128)S(1)} %get-tuple-element.10), custom_call_target="InvertDiagBlocksLowerTriangular" | custom-call | tf_op jit(solution)/shard_map/triangular_solve/custom-call.0 | solution.py:56
  180.3 47.1 %reduce-scatter.2.cloned.1.call-done = f32[512,128]{1,0:T(8,128)} async-done(((f32[8192,128]{1,0:T(8,128)}), f32[512,128]{1,0:T(8,128)}) %reduce-scatter.2.cloned.1.call-update) | async-done | bytes 262160 | tf_op jit(solution)/shard_map/reduce_scatter | solution.py:78
  (79 shorter events, 46.7 us)
Async XLA Ops:
  7.2 111.7 %copy-start = (bf16[512,128]{1,0:T(8,128)(2,1)S(1)}, bf16[512,128]{1,0:T(8,128)(2,1)}, u32[]{:S(2)}) copy-start(bf16[512,128]{1,0:T(8,128)(2,1)} %param.8) | copy-start | bytes 393220
  7.2 36.6 %copy-start.1 = (bf16[512,256]{1,0:T(8,128)(2,1)S(1)}, bf16[512,256]{1,0:T(8,128)(2,1)}, u32[]{:S(2)}) copy-start(bf16[512,256]{1,0:T(8,128)(2,1)} %param.7) | copy-start | bytes 786436
  7.2 220.2 %reduce-scatter.2.cloned.1.call-start = ((), (), s32[]{:S(2)}) async-start(), calls=%async_computation.1 | async-start | bytes 4456448 | tf_op jit(solution)/shard_map/reduce_scatter | solution.py:78
  7.2 12.5 %collective-permute-start = (bf16[512,256]{1,0:T(8,128)(2,1)}, bf16[512,256]{1,0:T(8,128)(2,1)S(1)}, u32[]{:S(2)}, u32[]{:S(2)}) collective-permute-start(bf16[512,256]{1,0:T(8,128)(2,1)} %param.7), channel_id=1, source_target_pairs={{0,32},{32,64},{64,96},{96,128},{128,160},{160,192},{192,224},{224... | collective-permute-start | bytes 786440 | tf_op jit(solution)/shard_map/ppermute | solution.py:22
  10.8 11.7 %collective-permute-start.1 = (bf16[512,256]{1,0:T(8,128)(2,1)}, bf16[512,256]{1,0:T(8,128)(2,1)S(1)}, u32[]{:S(2)}, u32[]{:S(2)}) collective-permute-start(bf16[512,256]{1,0:T(8,128)(2,1)} %param.7), channel_id=1, source_target_pairs={{0,480},{32,0},{64,32},{96,64},{128,96},{160,128},{192,160},{224,1... | collective-permute-start | bytes 786440 | tf_op jit(solution)/shard_map/ppermute | solution.py:27
  19.7 11.6 %collective-permute-start.2 = (bf16[512,256]{1,0:T(8,128)(2,1)S(1)}, bf16[512,256]{1,0:T(8,128)(2,1)S(1)}, u32[]{:S(2)}, u32[]{:S(2)}) collective-permute-start(bf16[512,256]{1,0:T(8,128)(2,1)S(1)} %collective-permute-done), channel_id=1, source_target_pairs={{0,32},{32,64},{64,96},{96,128},{128,160},{160,192},{192,224},{224... | collective-permute-start | bytes 786440 | tf_op jit(solution)/shard_map/ppermute | solution.py:22
  22.4 11.9 %collective-permute-start.3 = (bf16[512,256]{1,0:T(8,128)(2,1)S(1)}, bf16[512,256]{1,0:T(8,128)(2,1)S(1)}, u32[]{:S(2)}, u32[]{:S(2)}) collective-permute-start(bf16[512,256]{1,0:T(8,128)(2,1)S(1)} %collective-permute-done.1), channel_id=1, source_target_pairs={{0,480},{32,0},{64,32},{96,64},{128,96},{160,128},{192,160},{224,1... | collective-permute-start | bytes 786440 | tf_op jit(solution)/shard_map/ppermute | solution.py:27
  31.3 13.3 %collective-permute-start.4 = (bf16[512,256]{1,0:T(8,128)(2,1)S(1)}, bf16[512,256]{1,0:T(8,128)(2,1)S(1)}, u32[]{:S(2)}, u32[]{:S(2)}) collective-permute-start(bf16[512,256]{1,0:T(8,128)(2,1)S(1)} %collective-permute-done.2), channel_id=1, source_target_pairs={{0,32},{32,64},{64,96},{96,128},{128,160},{160,192},{192,224},{224... | collective-permute-start | bytes 786440 | tf_op jit(solution)/shard_map/ppermute | solution.py:22
  34.4 13.2 %collective-permute-start.5 = (bf16[512,256]{1,0:T(8,128)(2,1)S(1)}, bf16[512,256]{1,0:T(8,128)(2,1)S(1)}, u32[]{:S(2)}, u32[]{:S(2)}) collective-permute-start(bf16[512,256]{1,0:T(8,128)(2,1)S(1)} %collective-permute-done.3), channel_id=1, source_target_pairs={{0,480},{32,0},{64,32},{96,64},{128,96},{160,128},{192,160},{224,1... | collective-permute-start | bytes 786440 | tf_op jit(solution)/shard_map/ppermute | solution.py:27
  44.6 12.8 %collective-permute-start.6 = (bf16[512,256]{1,0:T(8,128)(2,1)S(1)}, bf16[512,256]{1,0:T(8,128)(2,1)S(1)}, u32[]{:S(2)}, u32[]{:S(2)}) collective-permute-start(bf16[512,256]{1,0:T(8,128)(2,1)S(1)} %collective-permute-done.4), channel_id=1, source_target_pairs={{0,32},{32,64},{64,96},{96,128},{128,160},{160,192},{192,224},{224... | collective-permute-start | bytes 786440 | tf_op jit(solution)/shard_map/ppermute | solution.py:22
  47.5 13.3 %collective-permute-start.7 = (bf16[512,256]{1,0:T(8,128)(2,1)S(1)}, bf16[512,256]{1,0:T(8,128)(2,1)S(1)}, u32[]{:S(2)}, u32[]{:S(2)}) collective-permute-start(bf16[512,256]{1,0:T(8,128)(2,1)S(1)} %collective-permute-done.5), channel_id=1, source_target_pairs={{0,480},{32,0},{64,32},{96,64},{128,96},{160,128},{192,160},{224,1... | collective-permute-start | bytes 786440 | tf_op jit(solution)/shard_map/ppermute | solution.py:27
  57.4 14.4 %collective-permute-start.8 = (bf16[512,256]{1,0:T(8,128)(2,1)S(1)}, bf16[512,256]{1,0:T(8,128)(2,1)S(1)}, u32[]{:S(2)}, u32[]{:S(2)}) collective-permute-start(bf16[512,256]{1,0:T(8,128)(2,1)S(1)} %collective-permute-done.6), channel_id=1, source_target_pairs={{0,32},{32,64},{64,96},{96,128},{128,160},{160,192},{192,224},{224... | collective-permute-start | bytes 786440 | tf_op jit(solution)/shard_map/ppermute | solution.py:22
  60.8 14.4 %collective-permute-start.9 = (bf16[512,256]{1,0:T(8,128)(2,1)S(1)}, bf16[512,256]{1,0:T(8,128)(2,1)S(1)}, u32[]{:S(2)}, u32[]{:S(2)}) collective-permute-start(bf16[512,256]{1,0:T(8,128)(2,1)S(1)} %collective-permute-done.7), channel_id=1, source_target_pairs={{0,480},{32,0},{64,32},{96,64},{128,96},{160,128},{192,160},{224,1... | collective-permute-start | bytes 786440 | tf_op jit(solution)/shard_map/ppermute | solution.py:27
  71.8 14.0 %collective-permute-start.10 = (bf16[512,256]{1,0:T(8,128)(2,1)S(1)}, bf16[512,256]{1,0:T(8,128)(2,1)S(1)}, u32[]{:S(2)}, u32[]{:S(2)}) collective-permute-start(bf16[512,256]{1,0:T(8,128)(2,1)S(1)} %collective-permute-done.8), channel_id=1, source_target_pairs={{0,32},{32,64},{64,96},{96,128},{128,160},{160,192},{192,224},{224... | collective-permute-start | bytes 786440 | tf_op jit(solution)/shard_map/ppermute | solution.py:22
  75.2 14.0 %collective-permute-start.11 = (bf16[512,256]{1,0:T(8,128)(2,1)S(1)}, bf16[512,256]{1,0:T(8,128)(2,1)S(1)}, u32[]{:S(2)}, u32[]{:S(2)}) collective-permute-start(bf16[512,256]{1,0:T(8,128)(2,1)S(1)} %collective-permute-done.9), channel_id=1, source_target_pairs={{0,480},{32,0},{64,32},{96,64},{128,96},{160,128},{192,160},{224,1... | collective-permute-start | bytes 786440 | tf_op jit(solution)/shard_map/ppermute | solution.py:27
  85.8 12.7 %collective-permute-start.12 = (bf16[512,256]{1,0:T(8,128)(2,1)S(1)}, bf16[512,256]{1,0:T(8,128)(2,1)S(1)}, u32[]{:S(2)}, u32[]{:S(2)}) collective-permute-start(bf16[512,256]{1,0:T(8,128)(2,1)S(1)} %collective-permute-done.10), channel_id=1, source_target_pairs={{0,32},{32,64},{64,96},{96,128},{128,160},{160,192},{192,224},{224... | collective-permute-start | bytes 786440 | tf_op jit(solution)/shard_map/ppermute | solution.py:22
  89.2 12.7 %collective-permute-start.13 = (bf16[512,256]{1,0:T(8,128)(2,1)S(1)}, bf16[512,256]{1,0:T(8,128)(2,1)S(1)}, u32[]{:S(2)}, u32[]{:S(2)}) collective-permute-start(bf16[512,256]{1,0:T(8,128)(2,1)S(1)} %collective-permute-done.11), channel_id=1, source_target_pairs={{0,480},{32,0},{64,32},{96,64},{128,96},{160,128},{192,160},{224,1... | collective-permute-start | bytes 786440 | tf_op jit(solution)/shard_map/ppermute | solution.py:27
  98.5 11.3 %collective-permute-start.14 = (bf16[512,256]{1,0:T(8,128)(2,1)S(1)}, bf16[512,256]{1,0:T(8,128)(2,1)S(1)}, u32[]{:S(2)}, u32[]{:S(2)}) collective-permute-start(bf16[512,256]{1,0:T(8,128)(2,1)S(1)} %collective-permute-done.12), channel_id=1, source_target_pairs={{0,32},{32,64},{64,96},{96,128},{128,160},{160,192},{192,224},{224... | collective-permute-start | bytes 786440 | tf_op jit(solution)/shard_map/ppermute | solution.py:22
  139.9 0.8 copy-start.2
  148.9 3.1 %collective-permute-start.15 = (f32[64,64]{1,0:T(8,128)S(1)}, f32[64,64]{1,0:T(8,128)S(1)}, u32[]{:S(2)}, u32[]{:S(2)}) collective-permute-start(f32[64,64]{1,0:T(8,128)S(1)} %fusion.10), channel_id=1, source_target_pairs={{0,1},{1,0},{2,3},{3,2},{4,5},{5,4},{6,7},{7,6},{8,9},{9,8},{10,11... | collective-permute-start | bytes 49160 | tf_op jit(solution)/shard_map/ppermute | solution.py:40
  159.5 7.5 %collective-permute-start.16 = (f32[64,64]{1,0:T(8,128)S(1)}, f32[64,64]{1,0:T(8,128)S(1)}, u32[]{:S(2)}, u32[]{:S(2)}) collective-permute-start(f32[64,64]{1,0:T(8,128)S(1)} %get-tuple-element.7), channel_id=1, source_target_pairs={{0,2},{1,3},{2,0},{3,1},{4,6},{5,7},{6,4},{7,5},{8,10},{9,11},{10,... | collective-permute-start | bytes 49160 | tf_op jit(solution)/shard_map/ppermute | solution.py:40
Sparse Core Ops, SparseCore 0:
  140.1 87.2 reduce-scatter.1
